TPU v7x, 32 devices: a whole 2x2x4 slice. The times are simulated.
32 devices in a mesh: seq: 16 (over z, x, core), tp: 2 (over y).
Axes of the slice: x: 2, y: 2, z: 4, core: 2. Of those that a mesh axis runs over, the one named last changes fastest.
Arguments:
- frames: bfloat16 [2, 4, 1024, 1024], P(None, 'tp', 'seq'), may hold values from -6 to 6
- time_embed: float32 [2, 4, 1024], replicated, may hold values from -6 to 6
- lengths: int32 [2, 4], replicated, may hold values from 1 to 1024, 2560 in all within a row
- w_query: bfloat16 [1024, 1024], P('seq', 'tp'), may hold values from -0.1875 to 0.1875
- w_key: bfloat16 [1024, 1024], P('seq', 'tp'), may hold values from -0.1875 to 0.1875
- w_value: bfloat16 [1024, 1024], P('seq', 'tp'), may hold values from -0.1875 to 0.1875
- w_out: bfloat16 [1024, 1024], P('tp', 'seq'), may hold values from -0.75 to 0.75
- w_up: bfloat16 [1024, 2048], P('seq', 'tp'), may hold values from -0.1875 to 0.1875
- w_down: bfloat16 [2048, 1024], P('tp', 'seq'), may hold values from -0.125 to 0.125
- w_mod: bfloat16 [1024, 6144], P('seq', 'tp'), may hold values from -0.1875 to 0.1875
- out_grad: bfloat16 [2, 4, 1024, 1024], P(None, 'tp', 'seq'), may hold values from -6 to 6
Outputs:
- layer_out: bfloat16 [2, 4, 1024, 1024], P(None, 'tp', 'seq')
- grad_input: bfloat16 [2, 4, 1024, 1024], P(None, 'tp', 'seq')
- grad_query: float32 [1024, 1024], P('seq', 'tp')
- grad_key: float32 [1024, 1024], P('seq', 'tp')
- grad_value: float32 [1024, 1024], P('seq', 'tp')
- grad_out: float32 [1024, 1024], P('tp', 'seq')
- grad_up: float32 [1024, 2048], P('seq', 'tp')
- grad_down: float32 [2048, 1024], P('tp', 'seq')
- grad_mod: float32 [1024, 6144], P('seq', 'tp')
Inputs may be any that keep to these rules, and one draw needn't show every extreme that they name: In every micro-batch the 4 lengths add up to 2560, and one item has exactly 1024 live frames.
All inputs are finite; a program needn't handle non-finite values.
Results may differ from a plain program's by a relative error of at most 0.024.
Values may be sent and summed in bfloat16 or wider, within the bound.
A program may use at most 384 MiB of HBM per device.

v0:
```python
from functools import partial
import math

import jax
import jax.numpy as jnp
from jax import lax
from jax.experimental import pallas as pl
from jax.experimental.pallas import tpu as pltpu
from jax.sharding import PartitionSpec as P

D = 1024
HEAD_DIM = 64
EPSILON = 1e-06
NEGATIVE = -1e30
BF = jnp.bfloat16
F32 = jnp.float32
HIGHEST = lax.Precision.HIGHEST
MESH = pl.DeviceIdType.MESH
ANY = pl.BlockSpec(memory_space=pl.ANY)
VMEM = pl.BlockSpec(memory_space=pltpu.VMEM)
LIMIT = 62 * 1024 * 1024


def nn(a, b):
    return lax.dot_general(a, b, (((1,), (0,)), ((), ())), preferred_element_type=F32)


def nt(a, b):
    return lax.dot_general(a, b, (((1,), (1,)), ((), ())), preferred_element_type=F32)


class Place:
    def __init__(self, S, T, I):
        self.S, self.T, self.I = S, T, I
        self.Z, self.R = S // 4, S // I
        self.Q = self.R // 2
        self.s, self.t = lax.axis_index("seq"), lax.axis_index("tp")
        self.z = lax.div(self.s, 4)
        self.x = lax.rem(lax.div(self.s, 2), 2)
        self.c = lax.rem(self.s, 2)
        self.i = lax.div(self.s, self.R)
        self.r = lax.rem(self.s, self.R)
        self.q = lax.div(self.r, 2)

    def at(self, z=None, x=None, c=None, t=None):
        z = self.z if z is None else z
        x = self.x if x is None else x
        c = self.c if c is None else c
        t = self.t if t is None else t
        return ((z * 2 + x) * 2 + c, t)

    def tp(self, k):
        return (self.s, lax.rem(self.t + k, self.T))

    def zs(self, k):
        return lax.rem(self.z + k, self.Z)

    def group(self, k, c=None):
        c = self.c if c is None else c
        return (self.i * self.R + lax.rem(self.q + k, self.Q) * 2 + c, self.t)


class Wires:
    def __init__(self, send, recv, local):
        self.send, self.recv, self.local = send, recv, local
        self.remote_count = self.local_count = 0
        self.sent = []

    def push(self, src, dst, device):
        n = self.remote_count
        self.remote_count += 1
        copy = pltpu.make_async_remote_copy(
            src_ref=src,
            dst_ref=dst,
            send_sem=self.send.at[n],
            recv_sem=self.recv.at[n],
            device_id=device,
            device_id_type=MESH,
        )
        copy.start()
        self.sent.append(copy)
        return copy

    def move(self, src, dst):
        n = self.local_count
        self.local_count += 1
        copy = pltpu.make_async_copy(src, dst, self.local.at[n])
        copy.start()
        return copy

    def close(self):
        for copy in self.sent:
            copy.wait_send()


def landed(copies):
    for copy in copies:
        copy.wait_recv()


def loop_group(place, first, body):
    total = place.R * place.T
    me = place.r * place.T + place.t

    def step(d, carry):
        other = lax.rem(me + d, total)
        body(d, place.i * place.R + lax.div(other, place.T), lax.rem(other, place.T))
        return carry

    lax.fori_loop(first, total, step, 0)


def greet(place):
    barrier = pltpu.get_barrier_semaphore()

    def signal(d, s, t):
        pl.semaphore_signal(barrier, inc=1, device_id=(s, t), device_id_type=MESH)

    for k in range(1, place.Z):
        signal(k, *place.at(z=place.zs(k)))
    loop_group(place, 1, signal)
    pl.semaphore_wait(barrier, place.Z - 1 + place.R * place.T - 1)


def spread_group(place, send, recv, src_of, dst):
    def copy(d, s, t):
        return pltpu.make_async_remote_copy(
            src_ref=src_of(t),
            dst_ref=dst.at[place.t, place.r],
            send_sem=send.at[d],
            recv_sem=recv.at[d],
            device_id=(s, t),
            device_id_type=MESH,
        )

    loop_group(place, 1, lambda d, s, t: copy(d, s, t).start())
    return lambda: loop_group(place, 1, lambda d, s, t: copy(d, s, t).wait())


class Phased:
    done = 0

    def upto(self, phase):
        while self.done <= phase:
            getattr(self, f"phase{self.done}")()
            self.done += 1


def split_rows(rs, quarters):
    upper = rs * quarters // 4 if rs * quarters // 4 % 16 == 0 else rs // 2
    return pl.ds(0, upper), pl.ds(upper, rs - upper)


class Gather(Phased):
    def __init__(self, place, wires, dst, quarters):
        self.p, self.w, self.dst = place, wires, dst
        self.upper, self.lower = split_rows(dst.shape[4], quarters)

    def phase0(self):
        p, w, dst = self.p, self.w, self.dst
        own = dst.at[0, p.z, p.x, p.c]
        self.along = [w.push(own, own, p.at(z=p.zs(k))) for k in range(1, p.Z)]

    def phase1(self):
        p, w, dst = self.p, self.w, self.dst
        landed(self.along)
        line = dst.at[0, :, p.x, p.c]
        self.sides = [
            w.push(
                dst.at[0, :, p.x, p.c, self.upper],
                dst.at[0, :, p.x, p.c, self.upper],
                p.at(x=1 - p.x),
            )
        ]
        for k in range(1, p.T):
            self.sides.append(
                w.push(
                    dst.at[0, :, p.x, p.c, self.lower],
                    dst.at[p.T - k, :, p.x, p.c, self.lower],
                    p.tp(k),
                )
            )
        self.cores = [w.push(line, line, p.at(c=1 - p.c))]

    def phase2(self):
        p, w, dst = self.p, self.w, self.dst
        landed(self.sides)
        self.last = []
        for k in range(1, p.T):
            self.last.append(
                w.push(
                    dst.at[0, :, :, p.c, self.upper],
                    dst.at[p.T - k, :, :, p.c, self.upper],
                    p.tp(k),
                )
            )
        part = dst.at[:, :, p.x, p.c, self.lower]
        self.last.append(w.push(part, part, p.at(x=1 - p.x)))
        part = dst.at[0, :, 1 - p.x, p.c, self.upper]
        self.cores.append(w.push(part, part, p.at(c=1 - p.c)))
        part = dst.at[pl.ds(1, p.T - 1), :, p.x, p.c, self.lower]
        self.cores.append(w.push(part, part, p.at(c=1 - p.c)))

    def phase3(self):
        p, w, dst = self.p, self.w, self.dst
        landed(self.last)
        part = dst.at[pl.ds(1, p.T - 1), :, :, p.c, self.upper]
        self.cores.append(w.push(part, part, p.at(c=1 - p.c)))
        part = dst.at[:, :, 1 - p.x, p.c, self.lower]
        self.cores.append(w.push(part, part, p.at(c=1 - p.c)))

    def phase4(self):
        landed(self.cores)


class Reduce(Phased):
    def __init__(self, place, wires, src, out, own, core_at, quarters, landing):
        self.p, self.w, self.src, self.out = place, wires, src, out
        self.own, self.core_at = own, core_at
        self.core, self.y_up, self.x_low, self.x_up, self.y_low, self.z_in = landing
        self.upper, self.lower = split_rows(own.shape[4], quarters)

    @staticmethod
    def landing(T, Z, rs, C, quarters):
        upper, lower = (part.size for part in split_rows(rs, quarters))
        return [
            pltpu.VMEM((T, Z, 2, rs, C), BF),
            pltpu.VMEM((T - 1, Z, 2, upper, C), BF),
            pltpu.VMEM((T, Z, lower, C), BF),
            pltpu.VMEM((Z, upper, C), BF),
            pltpu.VMEM((T - 1, Z, lower, C), BF),
            pltpu.VMEM((Z - 1, rs, C), BF),
        ]

    def phase0(self):
        p, w, src = self.p, self.w, self.src
        self.mine = None
        if self.own is not src:
            self.mine = w.move(src.at[:, :, :, pl.ds(p.c, 1)], self.own)
        self.pair = [w.push(src.at[:, :, :, 1 - p.c], self.core, p.at(c=1 - p.c))]

    def phase1(self):
        p, w, own, c = self.p, self.w, self.own, self.core_at
        if self.mine is not None:
            self.mine.wait()
        landed(self.pair)

        def add(n, carry):
            k, z = lax.div(n, p.Z), lax.rem(n, p.Z)
            for x in range(2):
                own[k, z, x, c] = own[k, z, x, c] + self.core[k, z, x]
            return carry

        lax.fori_loop(0, p.T * p.Z, add, 0)
        self.sides = [
            w.push(own.at[k, :, :, c, self.upper], self.y_up.at[k - 1], p.tp(k))
            for k in range(1, p.T)
        ]
        self.sides.append(
            w.push(own.at[:, :, 1 - p.x, c, self.lower], self.x_low, p.at(x=1 - p.x))
        )

    def phase2(self):
        p, w, own, c = self.p, self.w, self.own, self.core_at
        landed(self.sides)

        def add(z, carry):
            for x in range(2):
                total = own[0, z, x, c, self.upper].astype(F32)
                for k in range(1, p.T):
                    total = total + self.y_up[k - 1, z, x].astype(F32)
                own[0, z, x, c, self.upper] = total.astype(BF)
            for k in range(p.T):
                own[k, z, p.x, c, self.lower] = own[k, z, p.x, c, self.lower] + self.x_low[k, z]
            return carry

        lax.fori_loop(0, p.Z, add, 0)
        self.last = [w.push(own.at[0, :, 1 - p.x, c, self.upper], self.x_up, p.at(x=1 - p.x))]
        for k in range(1, p.T):
            self.last.append(
                w.push(own.at[k, :, p.x, c, self.lower], self.y_low.at[k - 1], p.tp(k))
            )

    def phase3(self):
        p, w, own, c = self.p, self.w, self.own, self.core_at
        landed(self.last)

        def add(z, carry):
            own[0, z, p.x, c, self.upper] = own[0, z, p.x, c, self.upper] + self.x_up[z]
            total = own[0, z, p.x, c, self.lower].astype(F32)
            for k in range(1, p.T):
                total = total + self.y_low[k - 1, z].astype(F32)
            own[0, z, p.x, c, self.lower] = total.astype(BF)
            return carry

        lax.fori_loop(0, p.Z, add, 0)
        self.along = [
            w.push(own.at[0, p.zs(k), p.x, c], self.z_in.at[k - 1], p.at(z=p.zs(k)))
            for k in range(1, p.Z)
        ]

    def phase4(self):
        p = self.p
        landed(self.along)
        total = self.own[0, p.z, p.x, self.core_at].astype(F32)
        for k in range(1, p.Z):
            total = total + self.z_in[k - 1].astype(F32)
        self.out[...] = total


def swap_items(place, wires, src, dst):
    p = place
    block = src if callable(src) else lambda n: src.at[n]
    own = wires.move(block(p.i), dst.at[p.i])
    copies = []
    for k in range(1, p.I):
        other = lax.rem(p.i + k, p.I)
        copies.append(wires.push(block(other), dst.at[p.i], (other * p.R + p.r, p.t)))
    return own, copies


def swap_pairs(v):
    lane = lax.broadcasted_iota(jnp.int32, v.shape, 1)
    return jnp.where(lax.rem(lane, 2) == 0, pltpu.roll(v, 127, 1), pltpu.roll(v, 1, 1))


def head_split(v):
    lane = lax.broadcasted_iota(jnp.int32, v.shape, 1)
    zero = jnp.zeros_like(v)
    return jnp.where(lane < HEAD_DIM, v, zero), jnp.where(lane < HEAD_DIM, zero, v)


def first_lane(rows):
    lane = lax.broadcasted_iota(jnp.int32, (rows, 128), 1)
    return jnp.where(lane == 0, 1.0, 0.0).astype(BF)


def attend_block(rows, cb, xm, weight, cos_ref, sin_ref, mask_ref, q_ref, k_ref, v_ref, att_ref, lse_ref):
    q_lin = nn(xm[0:rows, :], weight(0))
    k_lin = nn(xm, weight(1))
    v_ref[...] = nn(xm, weight(2)).astype(BF)
    ones = first_lane(rows)
    factor = HEAD_DIM**-0.5
    for p in range(cb // 128):
        lanes = slice(p * 128, p * 128 + 128)
        q2, k2 = q_lin[:, lanes], k_lin[:, lanes]
        q2 = (q2 * cos_ref[0:rows, :] + swap_pairs(q2) * sin_ref[0:rows, :]).astype(BF)
        q2 = q2 * jnp.asarray(factor, BF)
        k2 = (k2 * cos_ref[...] + swap_pairs(k2) * sin_ref[...]).astype(BF)
        q_ref[:, lanes] = q2
        k_ref[:, lanes] = k2
        k_long = jnp.concatenate([k2, mask_ref[...]], axis=1)
        v_turned = v_ref[:, lanes].T
        outs = []
        for h, q1 in enumerate(head_split(q2)):
            scores = nt(k_long, jnp.concatenate([q1, ones], axis=1))
            highest = jnp.max(scores, axis=0, keepdims=True)
            unnormed = jnp.exp(scores - highest)
            total = jnp.sum(unnormed, axis=0, keepdims=True)
            probs = (unnormed * (1.0 / total)).astype(BF)
            lse_ref[pl.ds(2 * p + h, 1), :] = highest + jnp.log(total)
            outs.append(nn(v_turned[h * HEAD_DIM : (h + 1) * HEAD_DIM], probs))
        att_ref[:, lanes] = jnp.concatenate(outs, axis=0).T.astype(BF)
    return nt(att_ref[...], weight(3))


def own_columns(place, time, rs):
    silu = (time / (1.0 + jnp.exp(-time))).astype(BF)
    feature = lax.broadcasted_iota(jnp.int32, (D, rs), 0)
    chosen = feature == lax.broadcasted_iota(jnp.int32, (D, rs), 1) + place.s * rs
    return nn(silu, jnp.where(chosen, 1.0, 0.0).astype(BF)).astype(BF)


def fill_tables(place, fl, length, cos_ref, sin_ref, mask_ref, live_ref):
    p = place
    lane = lax.broadcasted_iota(jnp.int32, (fl, 128), 1)
    row = lax.broadcasted_iota(jnp.int32, (fl, 128), 0)
    column = lax.div(lax.rem(lane, HEAD_DIM), 2).astype(F32)
    inverse = jnp.exp(column * (-2.0 * math.log(10000.0) / HEAD_DIM))
    sign = jnp.where(lax.rem(lane, 2) == 0, -1.0, 1.0)
    for g in range(p.R):
        r = lax.rem(p.q + g // 2, p.Q) * 2 + lax.rem(p.c + g % 2, 2)
        for n in range(p.I):
            at = pl.ds((g * p.I + n) * fl, fl)
            pos = row + fl * (n * p.R + r)
            angles = pos.astype(F32) * inverse
            cos_ref[at, :] = jnp.cos(angles)
            sin_ref[at, :] = jnp.sin(angles) * sign
            alive = pos < length
            mask_ref[at, :] = jnp.where((lane == 0) & ~alive, NEGATIVE, 0.0).astype(BF)
            if g == 0:
                live_ref[at, :] = jnp.where(alive, 1.0, 0.0)[:, 0:1]


def front_kernel(
    S, T, I, cb, hb,
    frames, cotangent, time_ref, lengths_ref, wq_ref, wk_ref, wv_ref, wo_ref, wu_ref, wd_ref, wm_ref,
    all_a, frames_in, xm_ref, q_ref, k_ref, v_ref, att_ref, lse_ref,
    mod_ref, layer_ref, grad_f, dmid_ref, dbranch_ref, dmod_ref, cos_ref, sin_ref, mask_ref,
    a_ref, f_ref, cot_in, parts, line_in, line_sum, parts_in, live_ref, branch_ref, mid_ref,
    normed_ref, mf_ref, mf_turned, db_ref, db_turned, out_sum, dmf_sum, stage,
    send, recv, local, row_send, row_recv, out_sem,
):
    p = Place(S, T, I)
    wires = Wires(send, recv, local)
    nq, nh = a_ref.shape[0], f_ref.shape[0]
    fl, rs = frames.shape[1], wq_ref.shape[0]
    rows, L = I * fl, I * fl * p.R
    micro, batch = lengths_ref.shape
    rows_own = I // micro
    for j in range(nq):
        cols = slice(j * cb, (j + 1) * cb)
        blocks = (wq_ref[:, cols], wk_ref[:, cols], wv_ref[:, cols], wo_ref[:, cols])
        a_ref[j, 0, p.z, p.x, p.c] = jnp.concatenate(blocks, axis=1)
    greet(p)
    chunks_a = [Gather(p, wires, a_ref.at[j], 2) for j in range(nq)]
    chunks_f = [Gather(p, wires, f_ref.at[j], 3) for j in range(nh)]
    chunks = chunks_a + chunks_f

    def upto(m, phase):
        if m < len(chunks):
            chunks[m].upto(phase)

    upto(0, 0)
    product = nn(own_columns(p, time_ref[...], rs), wm_ref[...])
    high = parts.shape[2]
    for item in range(micro * batch):
        m, b = divmod(item, batch)
        t, own = divmod(b, rows_own)
        for n in range(high):
            parts[t, m * rows_own + own, n : n + 1, :] = product[
                item : item + 1, n * 128 : (n + 1) * 128
            ]
    line = []
    for k in range(1, I):
        other = lax.rem(p.i + k, I)
        line.append(
            wires.push(parts.at[:, other], line_in.at[k - 1], (other * p.R + p.r, p.t))
        )
    for j in range(nh):
        cols = slice(j * hb, (j + 1) * hb)
        f_ref[j, 0, p.z, p.x, p.c] = jnp.concatenate([wu_ref[:, cols], wd_ref[:, cols]], axis=1)
    upto(0, 1)
    upto(1, 0)
    landed(line)
    for t in range(T):
        total = parts[t, p.i]
        for k in range(1, I):
            total = total + line_in[k - 1, t]
        line_sum[t] = total
    parts_in[p.t, p.r] = line_sum[p.t]
    group_done = spread_group(p, row_send, row_recv, lambda t: line_sum.at[t], parts_in)
    upto(0, 2)
    length = lengths_ref[lax.div(p.i, rows_own), p.t * rows_own + lax.rem(p.i, rows_own)]
    fill_tables(p, fl, length, cos_ref, sin_ref, mask_ref, live_ref)
    upto(1, 1)
    frames_own, frames_got = swap_items(p, wires, frames, frames_in)
    upto(0, 3)
    upto(1, 2)
    group_done()
    mod_ref[...] = jnp.zeros_like(mod_ref)
    for t in range(T):
        total = jnp.sum(parts_in[t], axis=0).astype(BF).astype(F32)
        for n in range(high):
            row, col = divmod((t * high + n) * 128, D)
            mod_ref[row : row + 1, col : col + 128] = total[n : n + 1]
    frames_own.wait()
    landed(frames_got)
    upto(2, 0)
    frame_rows = frames_in[...].reshape(rows, D).astype(F32)
    normed, _ = layer_stats(frame_rows)
    low = normed.astype(BF).astype(F32)
    xm_ref[0, 0] = (low * (1.0 + mod_ref[1:2, :]) + mod_ref[0:1, :]).astype(BF)
    sibling = p.group(0, 1 - p.c)
    across = [wires.push(xm_ref.at[0, 0], xm_ref.at[p.Q - k, 0], p.group(k)) for k in range(1, p.Q)]
    cores = [wires.push(xm_ref.at[0, 0], xm_ref.at[0, 1], sibling)]
    upto(2, 1)
    upto(3, 0)
    for k in range(1, p.Q):
        across[k - 1].wait_recv()
        cores.append(wires.push(xm_ref.at[p.Q - k, 0], xm_ref.at[p.Q - k, 1], sibling))
    upto(1, 3)
    landed(cores)

    cot_copies = []

    def ask_cotangent():
        own, got = swap_items(p, wires, cotangent, cot_in)
        cot_copies.extend([own, got])

    between = {
        0: lambda: (upto(2, 2), upto(3, 1), ask_cotangent()),
        1: lambda: (upto(3, 2),),
        2: lambda: (upto(2, 3),),
        3: lambda: (upto(3, 3),),
    }

    xm = xm_ref[...].reshape(L, D)
    copies = []
    for j in range(nq):
        chunks_a[j].upto(4)
        copies.append(wires.move(a_ref.at[j], all_a.at[j]))
        for t in range(T):
            n = j * T + t
            part = attend_block(
                rows, cb, xm,
                lambda b: a_ref[j, t, :, :, :, :, b * cb : (b + 1) * cb].reshape(D, cb),
                cos_ref, sin_ref, mask_ref,
                q_ref.at[n], k_ref.at[n], v_ref.at[n], att_ref.at[n], lse_ref.at[n],
            )
            if n == 0:
                branch_ref[...] = part
            else:
                branch_ref[...] += part
            between.get(n, tuple)()

    gate_attn, shift_ff = mod_ref[2:3, :], mod_ref[3:4, :]
    scale_ff, gate_ff = mod_ref[4:5, :], mod_ref[5:6, :]
    middle = (
        frames_in[...].reshape(rows, D).astype(F32)
        + gate_attn * live_ref[...] * branch_ref[...]
    )
    mid_ref[...] = middle
    normed, _ = layer_stats(middle)
    low = normed.astype(BF)
    normed_ref[...] = low
    modulated = (low.astype(F32) * (1.0 + scale_ff) + shift_ff).astype(BF)
    mf_ref[...] = modulated
    mf_turned[...] = modulated.T
    cot_copies[0].wait()
    landed(cot_copies[1])
    d_branch = (cot_in[...].reshape(rows, D).astype(F32) * gate_ff).astype(BF)
    db_ref[...] = d_branch
    db_turned[...] = d_branch.T

    pending = [None, None]
    for j in range(nh):
        chunks_f[j].upto(4)
        for t in range(T):
            n = j * T + t
            w_up = f_ref[j, t, :, :, :, :, 0:hb].reshape(D, hb)
            w_down = f_ref[j, t, :, :, :, :, hb : 2 * hb].reshape(D, hb)
            upper = nn(mf_ref[...], w_up)
            square = upper * upper
            slope = 0.7978845608
            tanh = jnp.tanh(slope * (upper + 0.044715 * upper * square))
            half = 0.5 * (1.0 + tanh)
            active = (upper * half).astype(BF)
            bend = half + 0.5 * upper * (1.0 - tanh * tanh) * (
                slope * (1.0 + 3 * 0.044715 * square)
            )
            d_upper = (nn(db_ref[...], w_down) * bend).astype(BF)
            if n == 0:
                out_sum[...] = nt(active, w_down)
                dmf_sum[...] = nt(d_upper, w_up)
            else:
                out_sum[...] += nt(active, w_down)
                dmf_sum[...] += nt(d_upper, w_up)
            slot = n % 2
            if pending[slot] is not None:
                pending[slot].wait()
            stage[slot, :, 0:hb] = nn(mf_turned[...], d_upper).astype(BF)
            stage[slot, :, hb : 2 * hb] = nn(db_turned[...], active).astype(BF)
            pending[slot] = pltpu.make_async_copy(stage.at[slot], grad_f.at[j, t], out_sem.at[slot])
            pending[slot].start()

    middle, branch_f = mid_ref[...], out_sum[...]
    layer_ref[...] = (middle + gate_ff * branch_f).astype(BF).reshape(layer_ref.shape)
    cot = cot_in[...].reshape(rows, D).astype(F32)
    normed, inverse = layer_stats(middle)
    dmf = dmf_sum[...]
    d_mid = cot + layer_back(normed, inverse, dmf * (1.0 + scale_ff))
    dmid_ref[...] = d_mid
    alive = d_mid * live_ref[...]
    dbranch_ref[...] = (alive * gate_attn).astype(BF)
    dmod_ref[...] = jnp.zeros_like(dmod_ref)
    dmod_ref[2:3, :] = jnp.sum(alive * branch_ref[...], axis=0, keepdims=True)
    dmod_ref[3:4, :] = jnp.sum(dmf, axis=0, keepdims=True)
    dmod_ref[4:5, :] = jnp.sum(dmf * normed_ref[...].astype(F32), axis=0, keepdims=True)
    dmod_ref[5:6, :] = jnp.sum(cot * branch_f, axis=0, keepdims=True)
    for copy in copies + [c for c in pending if c is not None]:
        copy.wait()
    wires.close()


def front_call(S, T, I, cb, hb, frames, cotangent, time, lengths, weights):
    w_query, w_up, w_mod = weights[0], weights[4], weights[6]
    rs = w_query.shape[0]
    nq, wide_a = w_query.shape[1] // cb, 4 * cb
    nh, wide_f = w_up.shape[1] // hb, 2 * hb
    fl = frames.shape[1]
    rows, Z, R = I * fl, S // 4, S // I
    Q, L, steps = R // 2, rows * R, nq * T
    high = w_mod.shape[1] // 128
    remote = 3 * (I - 1) + (nq + nh) * (Z + 2 * T + 4) + 2 * Q
    shape = jax.ShapeDtypeStruct
    vmem, dma = pltpu.VMEM, pltpu.SemaphoreType.DMA
    return pl.pallas_call(
        partial(front_kernel, S, T, I, cb, hb),
        out_shape=(
            shape((nq, T, Z, 2, 2, rs, wide_a), BF),
            shape(frames.shape, BF),
            shape((Q, 2, rows, D), BF),
            shape((steps, rows, cb), BF),
            shape((steps, L, cb), BF),
            shape((steps, L, cb), BF),
            shape((steps, rows, cb), BF),
            shape((steps, 8, rows), F32),
            shape((8, D), F32),
            shape(frames.shape, BF),
            shape((nh, T, D, wide_f), BF),
            shape((rows, D), F32),
            shape((rows, D), BF),
            shape((8, D), F32),
            shape((L, 128), F32),
            shape((L, 128), F32),
            shape((L, 128), BF),
        ),
        in_specs=[ANY] * 2 + [VMEM, pl.BlockSpec(memory_space=pltpu.SMEM)] + [VMEM] * 7,
        out_specs=(ANY,) + (VMEM,) * 9 + (ANY,) + (VMEM,) * 6,
        scratch_shapes=[
            vmem((nq, T, Z, 2, 2, rs, wide_a), BF),
            vmem((nh, T, Z, 2, 2, rs, wide_f), BF),
            vmem(frames.shape, BF),
            vmem((T, I, high, 128), F32),
            vmem((I - 1, T, high, 128), F32),
            vmem((T, high, 128), F32),
            vmem((T, R, high, 128), F32),
            vmem((rows, 1), F32),
            vmem((rows, D), F32),
            vmem((rows, D), F32),
            vmem((rows, D), BF),
            vmem((rows, D), BF),
            vmem((D, rows), BF),
            vmem((rows, D), BF),
            vmem((D, rows), BF),
            vmem((rows, D), F32),
            vmem((rows, D), F32),
            vmem((2, D, wide_f), BF),
            dma((remote,)),
            dma((remote,)),
            dma((2 + nq,)),
            dma((R * T,)),
            dma((R * T,)),
            dma((2,)),
        ],
        compiler_params=pltpu.CompilerParams(
            collective_id=0, has_side_effects=True, vmem_limit_bytes=LIMIT
        ),
        name="forward",
    )(frames, cotangent, time, lengths, *weights)


def attend_back_block(
    rows, cb, weight, wide, db_ref, xm_turned, db_turned, cos_ref, sin_ref, mask_ref,
    q_ref, k_ref, v_ref, att_ref, lse_ref, store,
):
    d_att = nn(db_ref[...], weight(3)).astype(BF)
    store(3, nn(db_turned[...], att_ref[...]))
    ones = first_lane(rows)
    factor = HEAD_DIM**-0.5
    dqs, dks, dvs = [], [], []
    for p in range(cb // 128):
        lanes = slice(p * 128, p * 128 + 128)
        q2, k2, v2 = q_ref[:, lanes], k_ref[:, lanes], v_ref[:, lanes]
        k_long = jnp.concatenate([k2, mask_ref[...]], axis=1)
        k_turned = k2.T
        dq_parts, ds_all, p_all = [], [], []
        q_heads, d_heads = head_split(q2), head_split(d_att[:, lanes])
        for h in range(2):
            scores = nt(k_long, jnp.concatenate([q_heads[h], ones], axis=1))
            probs = jnp.exp(scores - lse_ref[pl.ds(2 * p + h, 1), :])
            d_probs = nt(v2, d_heads[h])
            row_dot = jnp.sum(probs * d_probs, axis=0, keepdims=True)
            d_scores = (probs * (d_probs - row_dot)).astype(BF)
            dq_parts.append(nn(k_turned[h * HEAD_DIM : (h + 1) * HEAD_DIM], d_scores))
            ds_all.append(d_scores)
            p_all.append(probs.astype(BF))
        dk2 = nn(jnp.concatenate(ds_all, axis=1), jnp.concatenate(q_heads, axis=0))
        dv2 = nn(jnp.concatenate(p_all, axis=1), jnp.concatenate(d_heads, axis=0))
        dq2 = jnp.concatenate(dq_parts, axis=0).T * factor
        dqs.append(
            (dq2 * cos_ref[0:rows, :] - swap_pairs(dq2) * sin_ref[0:rows, :]).astype(BF)
        )
        dks.append((dk2 * cos_ref[...] - swap_pairs(dk2) * sin_ref[...]).astype(BF))
        dvs.append(dv2.astype(BF))
    dq, dk, dv = (jnp.concatenate(v, axis=1) for v in (dqs, dks, dvs))
    store(0, nn(xm_turned[:, 0:rows], dq))
    store(1, nn(xm_turned[...], dk))
    store(2, nn(xm_turned[...], dv))
    return nt(jnp.concatenate([dk, dv], axis=1), wide(1, 3)), nt(dq, weight(0))


def back_kernel(
    S, T, I, cb,
    layer, all_a, grad_f, k_all, v_all, xm_all, dmid, frames,
    q_ref, att_ref, lse_ref, mod_ref, db_ref, dmod_ref,
    cos_ref, sin_ref, mask_ref,
    layer_out, grads_out, rows_out, sum_a, sum_f,
    *scratch,
):
    nh, nq = grad_f.shape[0], all_a.shape[0]
    (xm_turned, db_turned, dx_sum, dx_ref, near, far, d_rows, group_in, group_sum, ga_ref,
     w_stage, k_stage, v_stage, in_sem, send, recv, local, row_send, row_recv) = scratch[:19]
    rest = scratch[19:]
    p = Place(S, T, I)
    wires = Wires(send, recv, local)
    Q, _, rows, _ = xm_all.shape
    L = Q * 2 * rows
    steps, slots = nq * T, w_stage.shape[0]

    def fetch(n):
        j, t = divmod(n, T)
        slot = n % slots
        copies = [
            pltpu.make_async_copy(all_a.at[j, t], w_stage.at[slot], in_sem.at[0, slot]),
            pltpu.make_async_copy(k_all.at[n], k_stage.at[slot], in_sem.at[1, slot]),
            pltpu.make_async_copy(v_all.at[n], v_stage.at[slot], in_sem.at[2, slot]),
        ]
        for copy in copies:
            copy.start()
        return copies

    xm_copy = wires.move(xm_all, dx_ref)
    fetched = fetch(0)
    greet(p)
    chunks_f, chunks_a = [], []
    for j in range(nh):
        own, landing, rest = rest[0], rest[1:7], rest[7:]
        chunks_f.append(Reduce(p, wires, grad_f.at[j], sum_f.at[j], own, 0, 2, landing))
    for j in range(nq):
        landing, rest = rest[:6], rest[6:]
        g = ga_ref.at[j]
        chunks_a.append(Reduce(p, wires, g, sum_a.at[j], g, p.c, 2, landing))
    chunks = chunks_f + chunks_a

    def upto(m, phase):
        if m < len(chunks):
            chunks[m].upto(phase)

    upto(0, 0)
    if nh > 1:
        upto(1, 0)
    xm_copy.wait()
    xm_turned[...] = dx_ref[...].reshape(L, D).T
    db_turned[...] = db_ref[...].T
    for m in range(nh):
        upto(m, 1)
    layer_own, layer_in = swap_items(p, wires, layer, layer_out)

    between = {
        0: lambda: None,
        1: lambda: (upto(nh, 0), upto(0, 2), upto(nh - 1, 2), upto(nh, 1)),
        2: lambda: (upto(0, 3), upto(nh - 1, 3)),
    }
    if nq == 1:
        between = {}

    for n in range(steps):
        j, t = divmod(n, T)
        slot = n % slots
        coming = fetch(n + 1) if slots == 2 and n + 1 < steps else None
        for copy in fetched:
            copy.wait()
        fetched = coming

        def store(b, value):
            ga_ref[j, t, :, :, :, :, b * cb : (b + 1) * cb] = value.astype(BF).reshape(
                ga_ref.shape[2:6] + (cb,)
            )

        dx, dx_own = attend_back_block(
            rows, cb,
            lambda b: w_stage[slot, :, b * cb : (b + 1) * cb],
            lambda b, e: w_stage[slot, :, b * cb : e * cb],
            db_ref, xm_turned, db_turned, cos_ref, sin_ref, mask_ref,
            q_ref.at[n], k_stage.at[slot], v_stage.at[slot], att_ref.at[n], lse_ref.at[n], store,
        )
        if n == 0:
            dx_sum[...] = dx
        else:
            dx_sum[...] += dx
        dx_sum[0:rows, :] += dx_own
        if slots == 1 and n + 1 < steps:
            fetched = fetch(n + 1)
        if n < steps - 1:
            between.get(n, tuple)()

    dx_ref[...] = dx_sum[...].astype(BF).reshape(dx_ref.shape)
    dmid_copy = wires.move(dmid, dx_sum.at[pl.ds(rows, rows)])
    fl = layer.shape[1]
    frame_copies = [
        wires.move(frames.at[n], xm_turned.at[pl.ds(n * fl, fl), pl.ds(0, D)]) for n in range(I)
    ]
    core = wires.push(dx_ref.at[:, 1], near, p.group(0, 1 - p.c))
    last = len(chunks) - 1
    upto(last, 0)
    core.wait_recv()
    across = []
    for k in range(1, Q):
        dx_ref[k, 0] = dx_ref[k, 0] + near[k]
        across.append(wires.push(dx_ref.at[k, 0], far.at[k - 1], p.group(k)))
    for m in range(last):
        upto(m, 2)
    upto(last, 1)
    for m in range(nh):
        upto(m, 3)

    for copy in frame_copies:
        copy.wait()
    normed, inverse = layer_stats(xm_turned[0:rows, 0:D].astype(F32))
    d_mod = dx_sum[0:rows, :] + near[0].astype(F32)
    for k in range(1, Q):
        across[k - 1].wait_recv()
        d_mod = d_mod + far[k - 1].astype(F32)
    incoming = layer_back(normed, inverse, d_mod * (1.0 + mod_ref[1:2, :]))
    dmid_copy.wait()
    dx_ref[0, 0] = (dx_sum[rows : 2 * rows, :] + incoming).astype(BF)
    grads_own, grads_in = swap_items(
        p, wires, lambda n: dx_ref.at[0, 0, pl.ds(n * fl, fl)], grads_out
    )
    high = d_rows.shape[1]
    first = [
        jnp.sum(d_mod, axis=0, keepdims=True),
        jnp.sum(d_mod * normed.astype(BF).astype(F32), axis=0, keepdims=True),
    ]
    for t in range(T):
        for n in range(high):
            row, col = divmod((t * high + n) * 128, D)
            value = first[row] if row < 2 else dmod_ref[row : row + 1, :]
            d_rows[t, n : n + 1, :] = value[:, col : col + 128]
    group_in[p.t, p.r] = d_rows[p.t]
    group_done = spread_group(p, row_send, row_recv, lambda t: d_rows.at[t], group_in)
    for m in range(last):
        upto(m, 3)
    group_done()
    for t in range(T):
        group_sum[t] = jnp.sum(group_in[t], axis=0)
    rows_own = wires.move(group_sum, rows_out.at[p.i])
    line = []
    for k in range(1, I):
        other = lax.rem(p.i + k, I)
        line.append(wires.push(group_sum, rows_out.at[p.i], (other * p.R + p.r, p.t)))
    upto(last, 2)
    for m in range(nh):
        upto(m, 4)
    upto(last, 3)
    for m in range(last + 1):
        upto(m, 4)
    landed(line)
    for own in (grads_own, layer_own, rows_own):
        own.wait()
    landed(grads_in)
    landed(layer_in)
    wires.close()


def back_call(
    S, T, I, cb, layer, all_a, grad_f, k, v, xm, d_mid, frames,
    q, att, lse, mod, d_branch, d_mod, cosine, sine, mask,
):
    nq, ca = all_a.shape[0], all_a.shape[3]
    nh, cf = grad_f.shape[0], grad_f.shape[6]
    rs = grad_f.shape[5]
    Z, Q, rows = S // 4, xm.shape[0], xm.shape[2]
    L = Q * 2 * rows
    high = 6 * D // T // 128
    slots = 2 if L <= 1024 else 1
    remote = 3 * (I - 1) + (nq + nh) * (Z + 2 * T + 2) + Q
    R = S // I
    shape = jax.ShapeDtypeStruct
    dma = pltpu.SemaphoreType.DMA
    scratch = [
        pltpu.VMEM((D, L), BF),
        pltpu.VMEM((D, rows), BF),
        pltpu.VMEM((L, D), F32),
        pltpu.VMEM((Q, 2, rows, D), BF),
        pltpu.VMEM((Q, rows, D), BF),
        pltpu.VMEM((Q - 1, rows, D), BF),
        pltpu.VMEM((T, high, 128), F32),
        pltpu.VMEM((T, R, high, 128), F32),
        pltpu.VMEM((T, high, 128), F32),
        pltpu.VMEM((nq, T, Z, 2, 2, rs, ca), BF),
        pltpu.VMEM((slots, D, ca), BF),
        pltpu.VMEM((slots, L, cb), BF),
        pltpu.VMEM((slots, L, cb), BF),
        dma((3, slots)),
        dma((remote,)),
        dma((remote,)),
        dma((5 + nh + I,)),
        dma((R * T,)),
        dma((R * T,)),
    ]
    for _ in range(nh):
        scratch += [pltpu.VMEM((T, Z, 2, 1, rs, cf), BF)] + Reduce.landing(T, Z, rs, cf, 2)
    for _ in range(nq):
        scratch += Reduce.landing(T, Z, rs, ca, 2)
    return pl.pallas_call(
        partial(back_kernel, S, T, I, cb),
        out_shape=(
            shape(layer.shape, BF),
            shape(layer.shape, BF),
            shape((I, T, high, 128), F32),
            shape((nq, rs, ca), F32),
            shape((nh, rs, cf), F32),
        ),
        in_specs=[ANY] * 8 + [VMEM] * 9,
        out_specs=(ANY, ANY, ANY, VMEM, VMEM),
        scratch_shapes=scratch,
        compiler_params=pltpu.CompilerParams(
            collective_id=1, has_side_effects=True, vmem_limit_bytes=LIMIT
        ),
        name="backward",
    )(
        layer, all_a, grad_f, k, v, xm, d_mid, frames,
        q, att, lse, mod, d_branch, d_mod, cosine, sine, mask,
    )


def layer_stats(values):
    center = values - jnp.mean(values, axis=-1, keepdims=True)
    inverse = lax.rsqrt(jnp.mean(center * center, axis=-1, keepdims=True) + EPSILON)
    return center * inverse, inverse


def layer_back(normed, inverse, incoming):
    return inverse * (
        incoming
        - jnp.mean(incoming, axis=-1, keepdims=True)
        - normed * jnp.mean(incoming * normed, axis=-1, keepdims=True)
    )


def finish_kernel(
    S, T, I, micro, time_ref, rows_ref, sum_a, sum_f, layer_in, grads_in,
    layer_ref, grads_ref, gq_ref, gk_ref, gv_ref, go_ref, gu_ref, gd_ref, gm_ref, items_ref,
):
    p = Place(S, T, I)
    nq, rs, wide_a = sum_a.shape
    nh, _, wide_f = sum_f.shape
    cb, hb = wide_a // 4, wide_f // 2
    layer_ref[...] = layer_in[...]
    grads_ref[...] = grads_in[...]
    for j in range(nq):
        for b, ref in enumerate((gq_ref, gk_ref, gv_ref, go_ref)):
            ref[:, j * cb : (j + 1) * cb] = sum_a[j, :, b * cb : (b + 1) * cb]
    for j in range(nh):
        gu_ref[:, j * hb : (j + 1) * hb] = sum_f[j, :, 0:hb]
        gd_ref[:, j * hb : (j + 1) * hb] = sum_f[j, :, hb : 2 * hb]
    high = rows_ref.shape[2]
    rows_own = I // micro
    for item in range(I * T):
        m, b = divmod(item, rows_own * T)
        i, t = m * rows_own + b % rows_own, b // rows_own
        for n in range(high):
            items_ref[item : item + 1, n * 128 : (n + 1) * 128] = rows_ref[i, t, n : n + 1, :]
    silu = own_columns(p, time_ref[...], rs).astype(F32)
    gm_ref[...] = lax.dot_general(
        silu, items_ref[...], (((0,), (0,)), ((), ())), precision=HIGHEST,
        preferred_element_type=F32,
    )


def finish_call(S, T, I, micro, time, rows, sum_a, sum_f, layer, grads, weights):
    shape = jax.ShapeDtypeStruct
    return pl.pallas_call(
        partial(finish_kernel, S, T, I, micro),
        out_shape=(shape(layer.shape, BF), shape(grads.shape, BF))
        + tuple(shape(w.shape, F32) for w in weights),
        in_specs=[VMEM] * 6,
        out_specs=(VMEM,) * 9,
        scratch_shapes=[pltpu.VMEM((I * T, weights[6].shape[1]), F32)],
        compiler_params=pltpu.CompilerParams(vmem_limit_bytes=LIMIT),
        name="finish",
    )(time, rows, sum_a, sum_f, layer, grads)


def per_device(
    S, T, frames, time_embed, lengths, w_query, w_key, w_value, w_out, w_up, w_down, w_mod, out_grad
):
    micro, rows_own, fl, _ = frames.shape
    batch = lengths.shape[1]
    I = micro * rows_own
    rs = w_query.shape[0]
    cb = min(256, w_query.shape[1])
    hb = min(512, w_up.shape[1])
    time = time_embed.reshape(micro * batch, D)
    weights = (w_query, w_key, w_value, w_out.T, w_up, w_down.T, w_mod)
    (
        all_a, frames_in, xm, q, k, v, att, lse, mod, layer, grad_f, d_mid, d_branch, d_rows,
        cosine, sine, mask,
    ) = front_call(
        S, T, I, cb, hb, frames.reshape(I, fl, D), out_grad.reshape(I, fl, D), time, lengths, weights
    )
    layer_out, grad_input, rows_in, sum_a, sum_f = back_call(
        S, T, I, cb, layer, all_a.reshape(all_a.shape[:2] + (D, 4 * cb)),
        grad_f.reshape((grad_f.shape[0], T, S // 4, 2, 2, rs, 2 * hb)), k, v, xm, d_mid,
        frames_in, q, att, lse, mod, d_branch, d_rows, cosine, sine, mask,
    )
    outs = finish_call(S, T, I, micro, time, rows_in, sum_a, sum_f, layer_out, grad_input, weights)
    layer_out, grad_input, g_query, g_key, g_value, g_out, g_up, g_down, g_mod = outs
    return (
        layer_out.reshape(frames.shape), grad_input.reshape(frames.shape),
        g_query, g_key, g_value, g_out.T, g_up, g_down.T, g_mod,
    )


def solution(mesh):
    S, T = mesh.shape["seq"], mesh.shape["tp"]
    rows = P(None, "tp", "seq", None)
    return jax.shard_map(
        partial(per_device, S, T),
        mesh=mesh,
        in_specs=(
            rows,
            P(),
            P(),
            P("seq", "tp"),
            P("seq", "tp"),
            P("seq", "tp"),
            P("tp", "seq"),
            P("seq", "tp"),
            P("tp", "seq"),
            P("seq", "tp"),
            rows,
        ),
        out_specs=(
            rows,
            rows,
            P("seq", "tp"),
            P("seq", "tp"),
            P("seq", "tp"),
            P("tp", "seq"),
            P("seq", "tp"),
            P("tp", "seq"),
            P("seq", "tp"),
        ),
        check_vma=False,
    )
```

profile of v0, /device:TPU:0, one launch (start us, length us, event | category | flops | bytes accessed | tf_op | source)
XLA Modules:
  0.0 245.3 jit_solution(3205225560803318646)
XLA Ops:
  0.6 1.4 reshape.39.time_ref
  2.0 130.6 %forward.1 = (bf16[2,2,4,2,2,64,1024]{6,5,4,3,2,1,0:T(8,128)(2,1)}, bf16[4,64,1024]{2,1,0:T(8,128)(2,1)}, bf16[2,2,256,1024]{3,2,1,0:T(8,128)(2,1)}, bf16[4,256,...) custom-call(bf16[4,64,1024]{2,1,0:T(8,128)(2,1)} %bitcast.12, ...), custom_call_target="tpu_custom_call" | custom-call | tf_op jit(solution)/shard_map/forward/pallas_call | solution.py:598
  132.6 108.4 %backward.1 = (bf16[4,64,1024]{2,1,0:T(8,128)(2,1)}, bf16[4,64,1024]{2,1,0:T(8,128)(2,1)}, f32[4,2,24,128]{3,2,1,0:T(8,128)}, f32[2,64,1024]{2,1,0:T(8,128)}, f32[2,64,1024]{2,1,0:T(8,128)}) custom-call(bf16[4,64,1024]{2,1,0:T(8,128)(2,1)} %get-tuple-element.40.layer, bf16[2,2,1024,1024]{3,2,1,0:T(8,128)(2,1)} %bitcast.10, ...), custom_call_target="tpu_custom_call" | custom-call | tf_op jit(solution)/shard_map/backward/pallas_call | solution.py:898
  241.0 4.1 %finish.1 = (bf16[4,64,1024]{2,1,0:T(8,128)(2,1)}, bf16[4,64,1024]{2,1,0:T(8,128)(2,1)}, f32[64,512]{1,0:T(8,128)}, f32[64,512]{1,0:T(8,128)}, f32[64,512]{1,0:T...) custom-call(f32[8,1024]{1,0:T(8,128)} %reshape.39.time_ref, ...), custom_call_target="tpu_custom_call" | custom-call | tf_op jit(solution)/shard_map/finish/pallas_call | solution.py:966
where the time goes:
time: 248 us; the launch traced here: 245 us
  Pallas kernels  243 us (98%)
    pallas_call x1, Pallas kernels, front_call(): pl.pallas_call(partial(front_kernel, S, T, I, cb, hb), out_shape=(shape((...  131 us
    pallas_call x1, Pallas kernels, back_call(): pl.pallas_call(partial(back_kernel, S, T, I, cb), out_shape=(shape(layer....  108 us

commit v1 on v0

--- a/solution.py
+++ b/solution.py
@@ -395,8 +395,9 @@
 def front_kernel(
     S, T, I, cb, hb,
     frames, cotangent, time_ref, lengths_ref, wq_ref, wk_ref, wv_ref, wo_ref, wu_ref, wd_ref, wm_ref,
-    all_a, frames_in, xm_ref, q_ref, k_ref, v_ref, att_ref, lse_ref,
-    mod_ref, layer_ref, grad_f, dmid_ref, dbranch_ref, dmod_ref, cos_ref, sin_ref, mask_ref,
+    all_a, xm_out, q_out, k_out, v_out, att_out, lse_out, grad_f, cos_out, sin_out, mask_out,
+    frames_in, mod_ref, layer_ref, dmid_ref, dbranch_ref, dmod_ref,
+    xm_ref, q_ref, k_ref, v_ref, att_ref, lse_ref, cos_ref, sin_ref, mask_ref,
     a_ref, f_ref, cot_in, parts, line_in, line_sum, parts_in, live_ref, branch_ref, mid_ref,
     normed_ref, mf_ref, mf_turned, db_ref, db_turned, out_sum, dmf_sum, stage,
     send, recv, local, row_send, row_recv, out_sem,
@@ -414,7 +415,7 @@
         a_ref[j, 0, p.z, p.x, p.c] = jnp.concatenate(blocks, axis=1)
     greet(p)
     chunks_a = [Gather(p, wires, a_ref.at[j], 2) for j in range(nq)]
-    chunks_f = [Gather(p, wires, f_ref.at[j], 3) for j in range(nh)]
+    chunks_f = [Gather(p, wires, f_ref.at[j], 2) for j in range(nh)]
     chunks = chunks_a + chunks_f
 
     def upto(m, phase):
@@ -441,7 +442,7 @@
         cols = slice(j * hb, (j + 1) * hb)
         f_ref[j, 0, p.z, p.x, p.c] = jnp.concatenate([wu_ref[:, cols], wd_ref[:, cols]], axis=1)
     upto(0, 1)
-    upto(1, 0)
+    frames_own, frames_got = swap_items(p, wires, frames, frames_in)
     landed(line)
     for t in range(T):
         total = parts[t, p.i]
@@ -453,10 +454,6 @@
     upto(0, 2)
     length = lengths_ref[lax.div(p.i, rows_own), p.t * rows_own + lax.rem(p.i, rows_own)]
     fill_tables(p, fl, length, cos_ref, sin_ref, mask_ref, live_ref)
-    upto(1, 1)
-    frames_own, frames_got = swap_items(p, wires, frames, frames_in)
-    upto(0, 3)
-    upto(1, 2)
     group_done()
     mod_ref[...] = jnp.zeros_like(mod_ref)
     for t in range(T):
@@ -466,7 +463,7 @@
             mod_ref[row : row + 1, col : col + 128] = total[n : n + 1]
     frames_own.wait()
     landed(frames_got)
-    upto(2, 0)
+    upto(1, 0)
     frame_rows = frames_in[...].reshape(rows, D).astype(F32)
     normed, _ = layer_stats(frame_rows)
     low = normed.astype(BF).astype(F32)
@@ -474,29 +471,40 @@
     sibling = p.group(0, 1 - p.c)
     across = [wires.push(xm_ref.at[0, 0], xm_ref.at[p.Q - k, 0], p.group(k)) for k in range(1, p.Q)]
     cores = [wires.push(xm_ref.at[0, 0], xm_ref.at[0, 1], sibling)]
-    upto(2, 1)
-    upto(3, 0)
+    upto(0, 3)
+    upto(1, 1)
+    upto(2, 0)
     for k in range(1, p.Q):
         across[k - 1].wait_recv()
         cores.append(wires.push(xm_ref.at[p.Q - k, 0], xm_ref.at[p.Q - k, 1], sibling))
-    upto(1, 3)
+    upto(1, 2)
+    upto(2, 1)
+    upto(3, 0)
     landed(cores)
 
-    cot_copies = []
+    cot_copies, steps = [], nq * T
 
     def ask_cotangent():
         own, got = swap_items(p, wires, cotangent, cot_in)
         cot_copies.extend([own, got])
 
     between = {
-        0: lambda: (upto(2, 2), upto(3, 1), ask_cotangent()),
-        1: lambda: (upto(3, 2),),
-        2: lambda: (upto(2, 3),),
-        3: lambda: (upto(3, 3),),
+        0: lambda: (upto(1, 3), upto(2, 2), upto(3, 1), upto(4, 0)),
+        1: lambda: (upto(2, 3), upto(3, 2), upto(4, 1), upto(5, 0)),
+        2: lambda: (upto(3, 3), upto(4, 2), upto(5, 1), ask_cotangent()),
+        3: lambda: (upto(4, 3), upto(5, 2)),
+        steps: lambda: (upto(5, 3),),
     }
+    if len(chunks) < 4:
+        between = {}
 
     xm = xm_ref[...].reshape(L, D)
-    copies = []
+    copies = [
+        wires.move(xm_ref, xm_out),
+        wires.move(cos_ref, cos_out),
+        wires.move(sin_ref, sin_out),
+        wires.move(mask_ref, mask_out),
+    ]
     for j in range(nq):
         chunks_a[j].upto(4)
         copies.append(wires.move(a_ref.at[j], all_a.at[j]))
@@ -513,7 +521,13 @@
             else:
                 branch_ref[...] += part
             between.get(n, tuple)()
-
+    if not cot_copies:
+        ask_cotangent()
+
+    for src, dst in (
+        (q_ref, q_out), (k_ref, k_out), (v_ref, v_out), (att_ref, att_out), (lse_ref, lse_out)
+    ):
+        copies.append(wires.move(src, dst))
     gate_attn, shift_ff = mod_ref[2:3, :], mod_ref[3:4, :]
     scale_ff, gate_ff = mod_ref[4:5, :], mod_ref[5:6, :]
     middle = (
@@ -563,6 +577,7 @@
             stage[slot, :, hb : 2 * hb] = nn(db_turned[...], active).astype(BF)
             pending[slot] = pltpu.make_async_copy(stage.at[slot], grad_f.at[j, t], out_sem.at[slot])
             pending[slot].start()
+            between.get(steps + n, tuple)()
 
     middle, branch_f = mid_ref[...], out_sum[...]
     layer_ref[...] = (middle + gate_ff * branch_f).astype(BF).reshape(layer_ref.shape)
@@ -595,30 +610,34 @@
     remote = 3 * (I - 1) + (nq + nh) * (Z + 2 * T + 4) + 2 * Q
     shape = jax.ShapeDtypeStruct
     vmem, dma = pltpu.VMEM, pltpu.SemaphoreType.DMA
+    kept = [
+        ((Q, 2, rows, D), BF),
+        ((steps, rows, cb), BF),
+        ((steps, L, cb), BF),
+        ((steps, L, cb), BF),
+        ((steps, rows, cb), BF),
+        ((steps, 8, rows), F32),
+        ((L, 128), F32),
+        ((L, 128), F32),
+        ((L, 128), BF),
+    ]
     return pl.pallas_call(
         partial(front_kernel, S, T, I, cb, hb),
-        out_shape=(
-            shape((nq, T, Z, 2, 2, rs, wide_a), BF),
+        out_shape=tuple(shape(*x) for x in [((nq, T, Z, 2, 2, rs, wide_a), BF)] + kept[:6])
+        + (shape((nh, T, D, wide_f), BF),)
+        + tuple(shape(*x) for x in kept[6:])
+        + (
             shape(frames.shape, BF),
-            shape((Q, 2, rows, D), BF),
-            shape((steps, rows, cb), BF),
-            shape((steps, L, cb), BF),
-            shape((steps, L, cb), BF),
-            shape((steps, rows, cb), BF),
-            shape((steps, 8, rows), F32),
             shape((8, D), F32),
             shape(frames.shape, BF),
-            shape((nh, T, D, wide_f), BF),
             shape((rows, D), F32),
             shape((rows, D), BF),
             shape((8, D), F32),
-            shape((L, 128), F32),
-            shape((L, 128), F32),
-            shape((L, 128), BF),
         ),
         in_specs=[ANY] * 2 + [VMEM, pl.BlockSpec(memory_space=pltpu.SMEM)] + [VMEM] * 7,
-        out_specs=(ANY,) + (VMEM,) * 9 + (ANY,) + (VMEM,) * 6,
-        scratch_shapes=[
+        out_specs=(ANY,) * 11 + (VMEM,) * 6,
+        scratch_shapes=[vmem(*x) for x in kept]
+        + [
             vmem((nq, T, Z, 2, 2, rs, wide_a), BF),
             vmem((nh, T, Z, 2, 2, rs, wide_f), BF),
             vmem(frames.shape, BF),
@@ -639,7 +658,7 @@
             vmem((2, D, wide_f), BF),
             dma((remote,)),
             dma((remote,)),
-            dma((2 + nq,)),
+            dma((11 + nq,)),
             dma((R * T,)),
             dma((R * T,)),
             dma((2,)),
@@ -729,9 +748,11 @@
         own, landing, rest = rest[0], rest[1:7], rest[7:]
         chunks_f.append(Reduce(p, wires, grad_f.at[j], sum_f.at[j], own, 0, 2, landing))
     for j in range(nq):
-        landing, rest = rest[:6], rest[6:]
-        g = ga_ref.at[j]
-        chunks_a.append(Reduce(p, wires, g, sum_a.at[j], g, p.c, 2, landing))
+        for h in (1, 0):
+            landing, rest = rest[:6], rest[6:]
+            cols = pl.ds(2 * cb * h, 2 * cb)
+            g = ga_ref.at[j, :, :, :, :, :, cols]
+            chunks_a.append(Reduce(p, wires, g, sum_a.at[j, :, cols], g, p.c, 2, landing))
     chunks = chunks_f + chunks_a
 
     def upto(m, phase):
@@ -742,19 +763,22 @@
     if nh > 1:
         upto(1, 0)
     xm_copy.wait()
+    db_turned[...] = db_ref[...].T
+    upto(0, 1)
+    for m in range(2, nh):
+        upto(m, 0)
     xm_turned[...] = dx_ref[...].reshape(L, D).T
-    db_turned[...] = db_ref[...].T
-    for m in range(nh):
+    for m in range(1, nh):
         upto(m, 1)
     layer_own, layer_in = swap_items(p, wires, layer, layer_out)
 
-    between = {
-        0: lambda: None,
-        1: lambda: (upto(nh, 0), upto(0, 2), upto(nh - 1, 2), upto(nh, 1)),
-        2: lambda: (upto(0, 3), upto(nh - 1, 3)),
-    }
-    if nq == 1:
-        between = {}
+    between = {}
+    if nq == 2 and T == 2 and nh == 4:
+        between = {
+            0: lambda: (upto(0, 2), upto(1, 2)),
+            1: lambda: (upto(4, 0), upto(5, 0), upto(2, 2), upto(3, 2), upto(4, 1), upto(5, 1)),
+            2: lambda: (upto(0, 3), upto(1, 3), upto(2, 3), upto(3, 3)),
+        }
 
     for n in range(steps):
         j, t = divmod(n, T)
@@ -794,14 +818,16 @@
     ]
     core = wires.push(dx_ref.at[:, 1], near, p.group(0, 1 - p.c))
     last = len(chunks) - 1
+    upto(last - 1, 0)
     upto(last, 0)
     core.wait_recv()
     across = []
     for k in range(1, Q):
         dx_ref[k, 0] = dx_ref[k, 0] + near[k]
         across.append(wires.push(dx_ref.at[k, 0], far.at[k - 1], p.group(k)))
-    for m in range(last):
+    for m in range(last - 1):
         upto(m, 2)
+    upto(last - 1, 1)
     upto(last, 1)
     for m in range(nh):
         upto(m, 3)
@@ -831,7 +857,7 @@
             d_rows[t, n : n + 1, :] = value[:, col : col + 128]
     group_in[p.t, p.r] = d_rows[p.t]
     group_done = spread_group(p, row_send, row_recv, lambda t: d_rows.at[t], group_in)
-    for m in range(last):
+    for m in range(last - 1):
         upto(m, 3)
     group_done()
     for t in range(T):
@@ -841,9 +867,11 @@
     for k in range(1, I):
         other = lax.rem(p.i + k, I)
         line.append(wires.push(group_sum, rows_out.at[p.i], (other * p.R + p.r, p.t)))
+    upto(last - 1, 2)
     upto(last, 2)
     for m in range(nh):
         upto(m, 4)
+    upto(last - 1, 3)
     upto(last, 3)
     for m in range(last + 1):
         upto(m, 4)
@@ -866,7 +894,7 @@
     L = Q * 2 * rows
     high = 6 * D // T // 128
     slots = 2 if L <= 1024 else 1
-    remote = 3 * (I - 1) + (nq + nh) * (Z + 2 * T + 2) + Q
+    remote = 3 * (I - 1) + (2 * nq + nh) * (Z + 2 * T + 2) + Q
     R = S // I
     shape = jax.ShapeDtypeStruct
     dma = pltpu.SemaphoreType.DMA
@@ -893,8 +921,8 @@
     ]
     for _ in range(nh):
         scratch += [pltpu.VMEM((T, Z, 2, 1, rs, cf), BF)] + Reduce.landing(T, Z, rs, cf, 2)
-    for _ in range(nq):
-        scratch += Reduce.landing(T, Z, rs, ca, 2)
+    for _ in range(2 * nq):
+        scratch += Reduce.landing(T, Z, rs, ca // 2, 2)
     return pl.pallas_call(
         partial(back_kernel, S, T, I, cb),
         out_shape=(
@@ -983,12 +1011,12 @@
     I = micro * rows_own
     rs = w_query.shape[0]
     cb = min(256, w_query.shape[1])
-    hb = min(512, w_up.shape[1])
+    hb = min(256, w_up.shape[1])
     time = time_embed.reshape(micro * batch, D)
     weights = (w_query, w_key, w_value, w_out.T, w_up, w_down.T, w_mod)
     (
-        all_a, frames_in, xm, q, k, v, att, lse, mod, layer, grad_f, d_mid, d_branch, d_rows,
-        cosine, sine, mask,
+        all_a, xm, q, k, v, att, lse, grad_f, cosine, sine, mask,
+        frames_in, mod, layer, d_mid, d_branch, d_rows,
     ) = front_call(
         S, T, I, cb, hb, frames.reshape(I, fl, D), out_grad.reshape(I, fl, D), time, lengths, weights
     )

time: 248 us -> 233 us (0.940)
  Pallas kernels: 243 us -> 228 us
    pallas_call x1, Pallas kernels: 131 us -> 117 us  [front_call(): pl.pallas_call(partial(front_kernel, S, T, I, cb, hb), out_shape=tuple((s...]
where the time goes in v1:
time: 233 us; the launch traced here: 230 us
  Pallas kernels  228 us (98%)
    pallas_call x1, Pallas kernels, front_call(): pl.pallas_call(partial(front_kernel, S, T, I, cb, hb), out_shape=tuple((s...  117 us
    pallas_call x1, Pallas kernels, back_call(): pl.pallas_call(partial(back_kernel, S, T, I, cb), out_shape=(shape(layer....  107 us

profile of v1, /device:TPU:0, one launch (start us, length us, event | category | flops | bytes accessed | tf_op | source)
XLA Modules:
  0.0 230.1 jit_solution(14546208995981316164)
XLA Ops:
  0.6 1.4 reshape.39.time_ref
  2.0 116.8 %forward.1 = (bf16[2,2,4,2,2,64,1024]{6,5,4,3,2,1,0:T(8,128)(2,1)}, bf16[2,2,256,1024]{3,2,1,0:T(8,128)(2,1)}, bf16[4,256,256]{2,1,0:T(8,128)(2,1)}, bf16[4,1024...) custom-call(bf16[4,64,1024]{2,1,0:T(8,128)(2,1)} %bitcast.12, ...), custom_call_target="tpu_custom_call" | custom-call | tf_op jit(solution)/shard_map/forward/pallas_call | solution.py:624
  118.8 107.0 %backward.1 = (bf16[4,64,1024]{2,1,0:T(8,128)(2,1)}, bf16[4,64,1024]{2,1,0:T(8,128)(2,1)}, f32[4,2,24,128]{3,2,1,0:T(8,128)}, f32[2,64,1024]{2,1,0:T(8,128)}, f32[4,64,512]{2,1,0:T(8,128)}) custom-call(bf16[4,64,1024]{2,1,0:T(8,128)(2,1)} %get-tuple-element.40.layer, bf16[2,2,1024,1024]{3,2,1,0:T(8,128)(2,1)} %bitcast.10, ...), custom_call_target="tpu_custom_call" | custom-call | tf_op jit(solution)/shard_map/backward/pallas_call | solution.py:926
  225.8 4.1 %finish.1 = (bf16[4,64,1024]{2,1,0:T(8,128)(2,1)}, bf16[4,64,1024]{2,1,0:T(8,128)(2,1)}, f32[64,512]{1,0:T(8,128)}, f32[64,512]{1,0:T(8,128)}, f32[64,512]{1,0:T...) custom-call(f32[8,1024]{1,0:T(8,128)} %reshape.39.time_ref, ...), custom_call_target="tpu_custom_call" | custom-call | tf_op jit(solution)/shard_map/finish/pallas_call | solution.py:994

commit v2 on v1

--- a/solution.py
+++ b/solution.py
@@ -365,6 +365,7 @@
 
 
 def own_columns(place, time, rs):
+    time = jnp.concatenate([time[m] for m in range(time.shape[0])], axis=0)
     silu = (time / (1.0 + jnp.exp(-time))).astype(BF)
     feature = lax.broadcasted_iota(jnp.int32, (D, rs), 0)
     chosen = feature == lax.broadcasted_iota(jnp.int32, (D, rs), 1) + place.s * rs
@@ -489,11 +490,11 @@
         cot_copies.extend([own, got])
 
     between = {
-        0: lambda: (upto(1, 3), upto(2, 2), upto(3, 1), upto(4, 0)),
-        1: lambda: (upto(2, 3), upto(3, 2), upto(4, 1), upto(5, 0)),
-        2: lambda: (upto(3, 3), upto(4, 2), upto(5, 1), ask_cotangent()),
-        3: lambda: (upto(4, 3), upto(5, 2)),
-        steps: lambda: (upto(5, 3),),
+        0: lambda: (upto(1, 3), upto(2, 2), upto(3, 1), upto(4, 0),),
+        1: lambda: (upto(2, 3), upto(3, 2), upto(4, 1), upto(5, 0),),
+        2: lambda: (upto(3, 3), upto(4, 2), upto(5, 1), ask_cotangent(),),
+        4: lambda: (upto(4, 3), upto(5, 2),),
+        7: lambda: (upto(5, 3),),
     }
     if len(chunks) < 4:
         between = {}
@@ -752,7 +753,7 @@
             landing, rest = rest[:6], rest[6:]
             cols = pl.ds(2 * cb * h, 2 * cb)
             g = ga_ref.at[j, :, :, :, :, :, cols]
-            chunks_a.append(Reduce(p, wires, g, sum_a.at[j, :, cols], g, p.c, 2, landing))
+            chunks_a.append(Reduce(p, wires, g, sum_a.at[j, :, cols], g, p.c, 3 if j == 1 else 2, landing))
     chunks = chunks_f + chunks_a
 
     def upto(m, phase):
@@ -921,8 +922,8 @@
     ]
     for _ in range(nh):
         scratch += [pltpu.VMEM((T, Z, 2, 1, rs, cf), BF)] + Reduce.landing(T, Z, rs, cf, 2)
-    for _ in range(2 * nq):
-        scratch += Reduce.landing(T, Z, rs, ca // 2, 2)
+    for j in range(2 * nq):
+        scratch += Reduce.landing(T, Z, rs, ca // 2, 3 if j // 2 == 1 else 2)
     return pl.pallas_call(
         partial(back_kernel, S, T, I, cb),
         out_shape=(
@@ -1012,7 +1013,7 @@
     rs = w_query.shape[0]
     cb = min(256, w_query.shape[1])
     hb = min(256, w_up.shape[1])
-    time = time_embed.reshape(micro * batch, D)
+    time = time_embed
     weights = (w_query, w_key, w_value, w_out.T, w_up, w_down.T, w_mod)
     (
         all_a, xm, q, k, v, att, lse, grad_f, cosine, sine, mask,

time: 233 us -> 229 us (0.983)
  Pallas kernels: 228 us -> 225 us
    pallas_call x1, Pallas kernels: 117 us -> 113 us  [front_call(): pl.pallas_call(partial(front_kernel, S, T, I, cb, hb), out_shape=tuple((s...]
where the time goes in v2:
time: 229 us; the launch traced here: 226 us
  Pallas kernels  225 us (98%)
    pallas_call x1, Pallas kernels, front_call(): pl.pallas_call(partial(front_kernel, S, T, I, cb, hb), out_shape=tuple((s...  113 us
    pallas_call x1, Pallas kernels, back_call(): pl.pallas_call(partial(back_kernel, S, T, I, cb), out_shape=(shape(layer....  108 us

profile of v2, /device:TPU:0, one launch (start us, length us, event | category | flops | bytes accessed | tf_op | source)
XLA Modules:
  0.0 226.2 jit_solution(4137848630570027593)
XLA Ops:
  0.6 113.2 %forward.1 = (bf16[2,2,4,2,2,64,1024]{6,5,4,3,2,1,0:T(8,128)(2,1)}, bf16[2,2,256,1024]{3,2,1,0:T(8,128)(2,1)}, bf16[4,256,256]{2,1,0:T(8,128)(2,1)}, bf16[4,1024...) custom-call(bf16[4,64,1024]{2,1,0:T(8,128)(2,1)} %bitcast.12, ...), custom_call_target="tpu_custom_call" | custom-call | tf_op jit(solution)/shard_map/forward/pallas_call | solution.py:625
  113.8 108.1 %backward.1 = (bf16[4,64,1024]{2,1,0:T(8,128)(2,1)}, bf16[4,64,1024]{2,1,0:T(8,128)(2,1)}, f32[4,2,24,128]{3,2,1,0:T(8,128)}, f32[2,64,1024]{2,1,0:T(8,128)}, f32[4,64,512]{2,1,0:T(8,128)}) custom-call(bf16[4,64,1024]{2,1,0:T(8,128)(2,1)} %get-tuple-element.40.layer, bf16[2,2,1024,1024]{3,2,1,0:T(8,128)(2,1)} %bitcast.10, ...), custom_call_target="tpu_custom_call" | custom-call | tf_op jit(solution)/shard_map/backward/pallas_call | solution.py:927
  221.9 4.1 %finish.1 = (bf16[4,64,1024]{2,1,0:T(8,128)(2,1)}, bf16[4,64,1024]{2,1,0:T(8,128)(2,1)}, f32[64,512]{1,0:T(8,128)}, f32[64,512]{1,0:T(8,128)}, f32[64,512]{1,0:T...) custom-call(f32[2,4,1024]{2,1,0:T(4,128)} %time_ref.3, ...), custom_call_target="tpu_custom_call" | custom-call | tf_op jit(solution)/shard_map/finish/pallas_call | solution.py:995

commit v3 on v2

--- a/solution.py
+++ b/solution.py
@@ -294,17 +294,34 @@
             return carry
 
         lax.fori_loop(0, p.Z, add, 0)
-        self.along = [
-            w.push(own.at[0, p.zs(k), p.x, c], self.z_in.at[k - 1], p.at(z=p.zs(k)))
-            for k in range(1, p.Z)
-        ]
+        if p.Z == 4:
+            near = p.z + 1 - 2 * lax.rem(p.z, 2)
+            self.along = [
+                w.push(own.at[0, near, p.x, c], self.z_in.at[0], p.at(z=near)),
+                w.push(own.at[0, 3 - p.z, p.x, c], self.z_in.at[1], p.at(z=near)),
+            ]
+        else:
+            self.along = [
+                w.push(own.at[0, p.zs(k), p.x, c], self.z_in.at[k - 1], p.at(z=p.zs(k)))
+                for k in range(1, p.Z)
+            ]
 
     def phase4(self):
+        p, w, own, c = self.p, self.w, self.own, self.core_at
+        landed(self.along)
+        self.across = []
+        if p.Z == 4:
+            far = p.zs(2)
+            own[0, far, p.x, c] = own[0, far, p.x, c] + self.z_in[1]
+            self.across.append(w.push(own.at[0, far, p.x, c], self.z_in.at[2], p.at(z=far)))
+
+    def phase5(self):
         p = self.p
-        landed(self.along)
+        landed(self.across)
+        blocks = (0, 2) if p.Z == 4 else range(p.Z - 1)
         total = self.own[0, p.z, p.x, self.core_at].astype(F32)
-        for k in range(1, p.Z):
-            total = total + self.z_in[k - 1].astype(F32)
+        for k in blocks:
+            total = total + self.z_in[k].astype(F32)
         self.out[...] = total
 
 
@@ -831,7 +848,7 @@
     upto(last - 1, 1)
     upto(last, 1)
     for m in range(nh):
-        upto(m, 3)
+        upto(m, 4)
 
     for copy in frame_copies:
         copy.wait()
@@ -870,12 +887,14 @@
         line.append(wires.push(group_sum, rows_out.at[p.i], (other * p.R + p.r, p.t)))
     upto(last - 1, 2)
     upto(last, 2)
-    for m in range(nh):
+    for m in range(last - 1):
         upto(m, 4)
     upto(last - 1, 3)
     upto(last, 3)
+    upto(last - 1, 4)
+    upto(last, 4)
     for m in range(last + 1):
-        upto(m, 4)
+        upto(m, 5)
     landed(line)
     for own in (grads_own, layer_own, rows_own):
         own.wait()

time: 229 us -> 226 us (0.987)
    pallas_call x1, Pallas kernels: 108 us -> 106 us  [back_call(): pl.pallas_call(partial(back_kernel, S, T, I, cb), out_shape=(shape(layer....]
where the time goes in v3:
time: 226 us; the launch traced here: 224 us
  Pallas kernels  223 us (99%)
    pallas_call x1, Pallas kernels, front_call(): pl.pallas_call(partial(front_kernel, S, T, I, cb, hb), out_shape=tuple((s...  113 us
    pallas_call x1, Pallas kernels, back_call(): pl.pallas_call(partial(back_kernel, S, T, I, cb), out_shape=(shape(layer....  106 us

profile of v3, /device:TPU:0, one launch (start us, length us, event | category | flops | bytes accessed | tf_op | source)
XLA Modules:
  0.0 223.6 jit_solution(12284445368381688755)
XLA Ops:
  0.6 113.2 %forward.1 = (bf16[2,2,4,2,2,64,1024]{6,5,4,3,2,1,0:T(8,128)(2,1)}, bf16[2,2,256,1024]{3,2,1,0:T(8,128)(2,1)}, bf16[4,256,256]{2,1,0:T(8,128)(2,1)}, bf16[4,1024...) custom-call(bf16[4,64,1024]{2,1,0:T(8,128)(2,1)} %bitcast.12, ...), custom_call_target="tpu_custom_call" | custom-call | tf_op jit(solution)/shard_map/forward/pallas_call | solution.py:642
  113.8 105.5 %backward.1 = (bf16[4,64,1024]{2,1,0:T(8,128)(2,1)}, bf16[4,64,1024]{2,1,0:T(8,128)(2,1)}, f32[4,2,24,128]{3,2,1,0:T(8,128)}, f32[2,64,1024]{2,1,0:T(8,128)}, f32[4,64,512]{2,1,0:T(8,128)}) custom-call(bf16[4,64,1024]{2,1,0:T(8,128)(2,1)} %get-tuple-element.40.layer, bf16[2,2,1024,1024]{3,2,1,0:T(8,128)(2,1)} %bitcast.10, ...), custom_call_target="tpu_custom_call" | custom-call | tf_op jit(solution)/shard_map/backward/pallas_call | solution.py:946
  219.3 4.1 %finish.1 = (bf16[4,64,1024]{2,1,0:T(8,128)(2,1)}, bf16[4,64,1024]{2,1,0:T(8,128)(2,1)}, f32[64,512]{1,0:T(8,128)}, f32[64,512]{1,0:T(8,128)}, f32[64,512]{1,0:T...) custom-call(f32[2,4,1024]{2,1,0:T(4,128)} %time_ref.3, ...), custom_call_target="tpu_custom_call" | custom-call | tf_op jit(solution)/shard_map/finish/pallas_call | solution.py:1014

commit v4 on v3

--- a/solution.py
+++ b/solution.py
@@ -152,17 +152,34 @@
 
 
 class Gather(Phased):
-    def __init__(self, place, wires, dst, quarters):
+    def __init__(self, place, wires, dst, quarters, paired):
         self.p, self.w, self.dst = place, wires, dst
+        self.paired = paired and place.Z == 4
         self.upper, self.lower = split_rows(dst.shape[4], quarters)
 
     def phase0(self):
         p, w, dst = self.p, self.w, self.dst
         own = dst.at[0, p.z, p.x, p.c]
-        self.along = [w.push(own, own, p.at(z=p.zs(k))) for k in range(1, p.Z)]
+        self.across = []
+        if self.paired:
+            self.across = [w.push(own, own, p.at(z=p.zs(2)))]
+            near = p.z + 1 - 2 * lax.rem(p.z, 2)
+            self.along = [w.push(own, own, p.at(z=near))]
+        else:
+            self.along = [w.push(own, own, p.at(z=p.zs(k))) for k in range(1, p.Z)]
+
+    def pass_on(self):
+        p, w, dst = self.p, self.w, self.dst
+        landed(self.across)
+        if self.paired and self.across:
+            near = p.z + 1 - 2 * lax.rem(p.z, 2)
+            far = dst.at[0, p.zs(2), p.x, p.c]
+            self.along.append(w.push(far, far, p.at(z=near)))
+        self.across = []
 
     def phase1(self):
         p, w, dst = self.p, self.w, self.dst
+        self.pass_on()
         landed(self.along)
         line = dst.at[0, :, p.x, p.c]
         self.sides = [
@@ -432,9 +449,13 @@
         blocks = (wq_ref[:, cols], wk_ref[:, cols], wv_ref[:, cols], wo_ref[:, cols])
         a_ref[j, 0, p.z, p.x, p.c] = jnp.concatenate(blocks, axis=1)
     greet(p)
-    chunks_a = [Gather(p, wires, a_ref.at[j], 2) for j in range(nq)]
-    chunks_f = [Gather(p, wires, f_ref.at[j], 2) for j in range(nh)]
+    chunks_a = [Gather(p, wires, a_ref.at[j], 2, False) for j in range(nq)]
+    chunks_f = [Gather(p, wires, f_ref.at[j], 2, True) for j in range(nh)]
     chunks = chunks_a + chunks_f
+
+    def pass_on(m):
+        if m < len(chunks):
+            chunks[m].pass_on()
 
     def upto(m, phase):
         if m < len(chunks):
@@ -490,11 +511,13 @@
     across = [wires.push(xm_ref.at[0, 0], xm_ref.at[p.Q - k, 0], p.group(k)) for k in range(1, p.Q)]
     cores = [wires.push(xm_ref.at[0, 0], xm_ref.at[0, 1], sibling)]
     upto(0, 3)
+    pass_on(1)
     upto(1, 1)
     upto(2, 0)
     for k in range(1, p.Q):
         across[k - 1].wait_recv()
         cores.append(wires.push(xm_ref.at[p.Q - k, 0], xm_ref.at[p.Q - k, 1], sibling))
+    pass_on(2)
     upto(1, 2)
     upto(2, 1)
     upto(3, 0)
@@ -507,9 +530,9 @@
         cot_copies.extend([own, got])
 
     between = {
-        0: lambda: (upto(1, 3), upto(2, 2), upto(3, 1), upto(4, 0),),
-        1: lambda: (upto(2, 3), upto(3, 2), upto(4, 1), upto(5, 0),),
-        2: lambda: (upto(3, 3), upto(4, 2), upto(5, 1), ask_cotangent(),),
+        0: lambda: (pass_on(3), upto(1, 3), upto(2, 2), upto(3, 1), upto(4, 0)),
+        1: lambda: (pass_on(4), upto(2, 3), upto(3, 2), upto(4, 1), upto(5, 0)),
+        2: lambda: (pass_on(5), upto(3, 3), upto(4, 2), upto(5, 1), ask_cotangent(),),
         4: lambda: (upto(4, 3), upto(5, 2),),
         7: lambda: (upto(5, 3),),
     }

time: 226 us -> 225 us (level)
    pallas_call x1, Pallas kernels: 106 us -> 103 us  [back_call(): pl.pallas_call(partial(back_kernel, S, T, I, cb), out_shape=(shape(layer....]
where the time goes in v4:
time: 225 us; the launch traced here: 222 us
  Pallas kernels  221 us (98%)
    pallas_call x1, Pallas kernels, front_call(): pl.pallas_call(partial(front_kernel, S, T, I, cb, hb), out_shape=tuple((s...  115 us
    pallas_call x1, Pallas kernels, back_call(): pl.pallas_call(partial(back_kernel, S, T, I, cb), out_shape=(shape(layer....  103 us

profile of v4, /device:TPU:0, one launch (start us, length us, event | category | flops | bytes accessed | tf_op | source)
XLA Modules:
  0.0 222.2 jit_solution(5564176707152243665)
XLA Ops:
  0.6 114.6 %forward.1 = (bf16[2,2,4,2,2,64,1024]{6,5,4,3,2,1,0:T(8,128)(2,1)}, bf16[2,2,256,1024]{3,2,1,0:T(8,128)(2,1)}, bf16[4,256,256]{2,1,0:T(8,128)(2,1)}, bf16[4,1024...) custom-call(bf16[4,64,1024]{2,1,0:T(8,128)(2,1)} %bitcast.12, ...), custom_call_target="tpu_custom_call" | custom-call | tf_op jit(solution)/shard_map/forward/pallas_call | solution.py:665
  115.3 102.6 %backward.1 = (bf16[4,64,1024]{2,1,0:T(8,128)(2,1)}, bf16[4,64,1024]{2,1,0:T(8,128)(2,1)}, f32[4,2,24,128]{3,2,1,0:T(8,128)}, f32[2,64,1024]{2,1,0:T(8,128)}, f32[4,64,512]{2,1,0:T(8,128)}) custom-call(bf16[4,64,1024]{2,1,0:T(8,128)(2,1)} %get-tuple-element.40.layer, bf16[2,2,1024,1024]{3,2,1,0:T(8,128)(2,1)} %bitcast.10, ...), custom_call_target="tpu_custom_call" | custom-call | tf_op jit(solution)/shard_map/backward/pallas_call | solution.py:969
  217.8 4.1 %finish.1 = (bf16[4,64,1024]{2,1,0:T(8,128)(2,1)}, bf16[4,64,1024]{2,1,0:T(8,128)(2,1)}, f32[64,512]{1,0:T(8,128)}, f32[64,512]{1,0:T(8,128)}, f32[64,512]{1,0:T...) custom-call(f32[2,4,1024]{2,1,0:T(4,128)} %time_ref.3, ...), custom_call_target="tpu_custom_call" | custom-call | tf_op jit(solution)/shard_map/finish/pallas_call | solution.py:1037
